TPU v7x, 256 devices: a whole 4x4x8 slice. The times are simulated.
256 devices in a mesh: dp: 32 (over y_lo, z, core), feat: 8 (over x, y_hi).
Axes of the slice: x: 4, y: 4 (y_hi: 2, y_lo: 2; y = y_hi * 2 + y_lo), z: 8, core: 2. Of those that a mesh axis runs over, the one named last changes fastest.
Arguments:
- image_feats: bfloat16 [32768, 1664], P(('dp', 'feat')), may hold values from -10 to 10
- text_feats: bfloat16 [32768, 1280], P(('dp', 'feat')), may hold values from -8 to 8
- image_head: bfloat16 [1664, 1280], replicated, may hold values from -0.09928379 to 0.09928379
- text_head: bfloat16 [1280, 1280], replicated, may hold values from -0.11320094 to 0.11320094
- sign_image: int32 [1664, 64], replicated, may hold values from 0 to 1
- sign_embed: int32 [1280, 64], replicated, may hold values from 0 to 1
- test_grads: bfloat16 [512, 4096], P(None, 'feat'), may hold values from -6 to 6
- subset_masks: int32 [256, 32768], P(None, ('dp', 'feat')), may hold values 0 or 1
Outputs:
- subset_scores: float32 [256, 512], P('dp', 'feat')
All inputs are finite; a program needn't handle non-finite values. No bound on the sum of `subset_masks` on one device may be relied on, other than what follows from the above.
Results may differ from a plain program's by a relative error of at most 0.0035.
The roundings to bfloat16 on the way count: a program that leaves them out, or rounds other values in their place, can miss the bound.
Values may be sent and summed in bfloat16 or wider, within the bound.
A program may use at most 128 MiB of HBM per device.

v0:
```python
import functools
import math

import jax
import jax.numpy as jnp
from jax import lax
from jax.experimental import pallas as pl
from jax.experimental.pallas import tpu as pltpu
from jax.sharding import PartitionSpec as P

X, Y = 4, 4
LANES = 128
LOG2E = math.log2(math.e)
MESH = pl.DeviceIdType.MESH
NT = (((1,), (1,)), ((), ()))


def dot_nt(a, b):
    return lax.dot_general(a, b, NT, preferred_element_type=jnp.float32)


def lse2(parts):
    top = functools.reduce(jnp.maximum, parts)
    total = functools.reduce(lambda a, b: a + b, [jnp.exp2(p - top) for p in parts])
    return top + jnp.log2(total)


class Names:
    def __init__(self):
        self.ids = {}

    def __call__(self, name):
        return self.ids.setdefault(name, len(self.ids))


PLANE = (
    (0, 0), (1, 0), (-1, 0), (0, 1),
    (0, -1), (1, 1), (1, -1), (-1, 1),
    (-1, -1), (2, 0), (0, 2), (2, 1),
    (2, -1), (1, 2), (-1, 2), (2, 2),
)


def kernel(
    cfg,
    feats_hbm, tfeats_hbm, ihead_hbm, thead_hbm, signi_hbm, signe_hbm, mask_hbm, tg_hbm,
    out_ref,
    feats, tfeats, ihead, thead, signi, signe, masks, tg,
    sgne, img, txt, logit, zr, tmax, tsum, imax, isum, rbuf, cbuf, rows_lse, msg, precv,
    fbuf, gall, frecv, maskall, phi, tot, crecv, pk, prs, acc2, zrs,
    send_sem, recv_sem, load_sem,
):
    pairs, Z, TB = cfg["pairs"], cfg["Z"], 2 * cfg["pairs"]
    IB = 4 * pairs
    half, quarter = pairs // 2, pairs // 4
    HZ = Z // 2
    order = [0] + [d for k in range(1, HZ) for d in (k, -k)] + [HZ]
    dp, feat = lax.axis_index("dp"), lax.axis_index("feat")
    c = dp & 1
    z = (dp >> 1) & (Z - 1)
    yl = dp >> (Z.bit_length())
    x = feat >> 1
    y = ((feat & 1) << 1) + yl

    xs = [(x + d) & (X - 1) for d in range(X)]
    ys = [(y + d) & (Y - 1) for d in range(Y)]
    zs = [(z + d) & (Z - 1) for d in range(Z)]
    cs = [c, 1 - c]
    x_part = [v << 1 for v in xs]
    y_feat = [v >> 1 for v in ys]
    y_dp = [(v & 1) << (Z.bit_length()) for v in ys]
    z_part = [v << 1 for v in zs]

    def dev(dx=0, dy=0, dz=0, dc=0):
        return {
            "dp": y_dp[dy % Y] + z_part[dz % Z] + cs[dc % 2],
            "feat": x_part[dx % X] + y_feat[dy % Y],
        }

    def image_slot(dx, dy):
        return (xs[dx % X] << 2) + ys[dy % Y]

    def text_slot(dz, dc):
        return cs[dc % 2] * Z + zs[dz % Z]

    plane = PLANE[1:]
    line = [(dz, dc) for dc in range(2) for dz in range(Z) if (dz, dc) != (0, 0)]
    mates = [(dx, 2 * h) for dx in range(X) for h in range(2) if (dx, h) != (0, 0)]

    loads = [
        pltpu.make_async_copy(src, dst, load_sem.at[i])
        for i, (src, dst) in enumerate(
            (
                (tfeats_hbm, tfeats), (thead_hbm, thead), (feats_hbm, feats),
                (ihead_hbm, ihead), (signe_hbm, signe), (signi_hbm, signi),
                (mask_hbm, masks), (tg_hbm, tg),
            )
        )
    ]
    for load in loads:
        load.start()

    barrier = pltpu.get_barrier_semaphore()
    for dx, dy in plane:
        pl.semaphore_signal(barrier, inc=1, device_id=dev(dx, dy), device_id_type=MESH)
    for dz, dc in line:
        pl.semaphore_signal(barrier, inc=1, device_id=dev(0, 0, dz, dc), device_id_type=MESH)

    names = Names()
    started = []

    def send(name, src, dst, to):
        i = names(name)
        copy = pltpu.make_async_remote_copy(
            src_ref=src, dst_ref=dst, send_sem=send_sem.at[i], recv_sem=recv_sem.at[i],
            device_id=to, device_id_type=MESH,
        )
        copy.start()
        started.append(copy)

    def recv(name, dst):
        i = names(name)
        pltpu.make_async_remote_copy(
            src_ref=dst, dst_ref=dst, send_sem=send_sem.at[i], recv_sem=recv_sem.at[i],
            device_id=dev(1), device_id_type=MESH,
        ).wait_recv()

    def drain():
        for copy in started:
            copy.wait_send()
        started.clear()

    def wrap(d, n):
        return (d + n // 2 - 1) % n - (n // 2 - 1)

    def image(dx, dy, r0, n):
        k = PLANE.index((wrap(dx, X), wrap(dy, Y)))
        return img.at[pl.ds(k * pairs + r0, n), :]

    def text(dz, dc, r0, n):
        k = order.index(wrap(dz, Z)) * 2 + dc % 2
        return txt.at[pl.ds(k * pairs + r0, n), :]

    def project(feats_ref, head_ref):
        proj = jnp.dot(feats_ref[...], head_ref[...], preferred_element_type=jnp.float32)
        length = jnp.sqrt(jnp.sum(proj * proj, axis=1, keepdims=True) + 1e-06)
        return (proj / length).astype(jnp.bfloat16), length

    def text_pieces(s, up):
        if s < HZ - 1:
            return (0, 1)
        return (0,) if up else (1,)

    def text_send(s, h):
        for up, step in ((True, 1), (False, -1)):
            if h in text_pieces(s, up):
                src = text(-s * step, 0, h * half, half)
                dst = text(-(s + 1) * step, 0, h * half, half)
                send(f"z{step}{s}{h}", src, dst, dev(0, 0, step, 0))

    def text_recv(s, h):
        for up, step in ((True, 1), (False, -1)):
            if h in text_pieces(s, up):
                recv(f"z{step}{s}{h}", text(-(s + 1) * step, 0, h * half, half))

    def text_share(dz):
        send(f"s{dz}", text(dz, 0, 0, pairs), text(dz, 1, 0, pairs), dev(0, 0, 0, 1))

    def text_shared(dz):
        recv(f"s{dz}", text(dz, 1, 0, pairs))

    def axes(which):
        return ((1, 0), (0, 1)) if which == 0 else ((0, 1), (1, 0))

    def at(which, a, b, r0, n):
        (fx, fy), (gx, gy) = axes(which)
        return image(fx * a + gx * b, fy * a + gy * b, which * half + r0, n)

    def part(d):
        return 0 if d == 1 else quarter

    def first_send(which):
        (fx, fy), _ = axes(which)
        for d in (1, -1):
            src, dst = at(which, 0, 0, 0, half), at(which, -d, 0, 0, half)
            send(f"f{which}{d}", src, dst, dev(fx * d, fy * d))

    def first_forward(which):
        (fx, fy), _ = axes(which)
        for d in (1, -1):
            recv(f"f{which}{d}", at(which, -d, 0, 0, half))
            src = at(which, -d, 0, part(d), quarter)
            send(f"F{which}{d}", src, at(which, 2, 0, part(d), quarter), dev(fx * d, fy * d))

    def first_last(which):
        for d in (1, -1):
            recv(f"F{which}{d}", at(which, 2, 0, part(d), quarter))

    def second_send(which, a):
        _, (gx, gy) = axes(which)
        for d in (1, -1):
            src, dst = at(which, a, 0, 0, half), at(which, a, -d, 0, half)
            send(f"g{which}{a}{d}", src, dst, dev(gx * d, gy * d))

    def second_forward(which, a):
        _, (gx, gy) = axes(which)
        for d in (1, -1):
            recv(f"g{which}{a}{d}", at(which, a, -d, 0, half))
            src = at(which, a, -d, part(d), quarter)
            send(f"G{which}{a}{d}", src, at(which, a, 2, part(d), quarter), dev(gx * d, gy * d))

    def second_last(which, a):
        for d in (1, -1):
            recv(f"G{which}{a}{d}", at(which, a, 2, part(d), quarter))

    scale = 100.0 * LOG2E

    def tile(t, ic):
        rows = pl.ds(t * TB if isinstance(t, int) else pl.multiple_of(t * TB, TB), TB)
        cols = pl.ds(ic * IB if isinstance(ic, int) else pl.multiple_of(ic * IB, IB), IB)
        block = dot_nt(txt[rows, :], img[cols, :]) * scale
        logit[ic, rows, :] = block
        deep = block.reshape(TB // 8, 8, IB)
        old = imax[ic]
        new = jnp.maximum(old, jnp.max(deep, axis=0))
        isum[ic] = isum[ic] * jnp.exp2(old - new) + jnp.sum(jnp.exp2(deep - new[None]), axis=0)
        imax[ic] = new
        parts = [block[:, k : k + LANES] for k in range(0, IB, LANES)]
        old = tmax[rows, :]
        new = functools.reduce(jnp.maximum, parts, old)
        tsum[rows, :] = functools.reduce(
            lambda a, b: a + b,
            [jnp.exp2(p - new) for p in parts],
            tsum[rows, :] * jnp.exp2(old - new),
        )
        tmax[rows, :] = new

    def tiles(n, at_step):
        def body(i, carry):
            for t, ic in at_step(i):
                tile(t, ic)
            return carry

        lax.fori_loop(0, n, body, 0)

    n_t = len(order)

    loads[0].wait()
    loads[1].wait()
    own_text, _ = project(tfeats, thead)
    txt[0:pairs, :] = own_text
    pl.semaphore_wait(barrier, len(plane) + len(line))
    text_send(0, 0)
    text_send(0, 1)
    text_share(0)
    loads[2].wait()
    loads[3].wait()
    own_image, length = project(feats, ihead)
    img[0:pairs, :] = own_image
    for which in (0, 1):
        first_send(which)
    for which in (0, 1):
        second_send(which, 0)

    for i in (4, 5, 6, 7):
        loads[i].wait()
    sgne[...] = (2 * signe[...] - 1).astype(jnp.bfloat16)
    norm = jnp.broadcast_to(length, (pairs, LANES)).T[0:1, :]
    izr = dot_nt(sgne[...], own_image)
    own_zr = dot_nt(sgne[...], own_text).astype(jnp.bfloat16).astype(jnp.float32)
    prod = own_image.astype(jnp.float32) * own_text.astype(jnp.float32)
    lanes = functools.reduce(
        lambda a, b: a + b, [prod[:, k : k + LANES] for k in range(0, prod.shape[1], LANES)]
    )
    own_logit = 100.0 * jnp.sum(lanes.T, axis=0, keepdims=True)
    fbuf[...] = dot_nt((2 * signi[...] - 1).astype(jnp.bfloat16), feats[...])
    mine = pl.ds(pl.multiple_of(feat * pairs, pairs), pairs)
    maskall[:, mine] = masks[...].astype(jnp.bfloat16)
    frecv[feat] = fbuf[pl.ds(pl.multiple_of(feat * 8, 8), 8), :]
    tmax[...] = jnp.full(tmax.shape, -1e30, jnp.float32)
    tsum[...] = jnp.zeros(tsum.shape, jnp.float32)
    imax[...] = jnp.full(imax.shape, -1e30, jnp.float32)
    isum[...] = jnp.zeros(isum.shape, jnp.float32)

    for which in (0, 1):
        first_forward(which)
        second_send(which, -1)
        second_send(which, 1)
    for h in (0, 1):
        text_recv(0, h)
        text_send(1, h)
    text_share(1)
    text_share(-1)
    for which in (0, 1):
        second_forward(which, 0)
    for which in (0, 1):
        first_last(which)
        second_send(which, 2)
    for dz in (0, 1, -1):
        text_shared(dz)
    tiles(3, lambda i: [(i, 0)])
    for h in (0, 1):
        text_recv(1, h)
        text_send(2, h)
    text_share(2)
    text_share(-2)
    for which in (0, 1):
        for a in (-1, 1):
            second_forward(which, a)
    text_shared(2)
    text_shared(-2)
    tiles(2, lambda i: [(i + 3, 0), (i + 3, 1)])
    text_recv(2, 0)
    text_send(3, 0)
    tiles(3, lambda i: [(i, 1)])
    text_recv(2, 1)
    text_send(3, 1)
    text_share(3)
    text_share(-3)
    for which in (0, 1):
        second_forward(which, 2)
    text_shared(3)
    text_shared(-3)
    tiles(2, lambda i: [(i + 5, 0), (i + 5, 1)])
    for which in (0, 1):
        for a in (0, 1):
            second_last(which, a)
    tiles(n_t - 1, lambda i: [(i, 2)])
    text_recv(3, 0)
    text_recv(3, 1)
    text_share(HZ)
    for which in (0, 1):
        for a in (-1, 2):
            second_last(which, a)
    tiles((n_t - 2) // 2, lambda i: [(2 * i, 3), (2 * i + 1, 3)])
    text_shared(HZ)
    tiles(1, lambda i: [(n_t - 2, 3), (n_t - 1, 0), (n_t - 1, 1), (n_t - 1, 2), (n_t - 1, 3)])

    for dx, dy in mates:
        to = dev(dx, dy)
        send(f"m{dx}{dy}", maskall.at[:, mine], maskall.at[:, mine], to)
        send(f"r{dx}{dy}", fbuf.at[pl.ds(to["feat"] * 8, 8), :], frecv.at[feat], to)

    for k, (dx, dy) in enumerate(PLANE):
        ic, cols = k // 4, slice(k % 4 * LANES, (k % 4 + 1) * LANES)
        high = imax[ic, :, cols]
        top = jnp.max(high, axis=0, keepdims=True)
        total = jnp.sum(isum[ic, :, cols] * jnp.exp2(high - top), axis=0, keepdims=True)
        rbuf[0, pl.ds(image_slot(dx, dy), 1), :] = top + jnp.log2(total)
    for k, (dx, dy) in enumerate(plane):
        send(f"R{k}", rbuf.at[0], rbuf.at[k + 1], dev(dx, dy))
    texts = [(dz, dc) for dz in order for dc in range(2)]
    for b, (dz, dc) in enumerate(texts):
        rows = slice(b * LANES, (b + 1) * LANES)
        high = tmax[rows, :].T
        top = jnp.max(high, axis=0, keepdims=True)
        total = jnp.sum(tsum[rows, :].T * jnp.exp2(high - top), axis=0, keepdims=True)
        cbuf[0, pl.ds(text_slot(dz, dc), 1), :] = top + jnp.log2(total)
    for k, (dz, dc) in enumerate(line):
        send(f"C{k}", cbuf.at[0], cbuf.at[k + 1], dev(0, 0, dz, dc))

    for t in range(n_t // 2):
        rows = slice(t * 2 * TB, (t + 1) * 2 * TB)
        zr[t] = dot_nt(sgne[...], txt[rows, :]).astype(jnp.bfloat16)
    drain()

    for k in range(len(plane)):
        recv(f"R{k}", rbuf.at[k + 1])
    rbuf[0] = lse2([rbuf[k] for k in range(len(plane) + 1)])
    for k, (dx, dy) in enumerate(PLANE):
        cols = slice(k % 4 * LANES, (k % 4 + 1) * LANES)
        rows_lse[k // 4, :, cols] = rbuf[0, pl.ds(image_slot(dx, dy), 1), :]
    for k in range(len(line)):
        recv(f"C{k}", cbuf.at[k + 1])
    cbuf[0] = lse2([cbuf[k] for k in range(len(line) + 1)])
    for b, (dz, dc) in enumerate(texts):
        col = cbuf[0, pl.ds(text_slot(dz, dc), 1), :]
        tmax[b * LANES : (b + 1) * LANES, :] = jnp.broadcast_to(col, (LANES, LANES)).T

    for ic in (3, 2, 1, 0):
        row = rows_lse[ic]

        def second_pass(t, carry):
            acc, radial = carry
            rows = pl.ds(pl.multiple_of(t * 2 * TB, 2 * TB), 2 * TB)
            block = logit[ic, rows, :]
            col = tmax[rows, :]
            col = jnp.concatenate([col] * (IB // LANES), axis=1)
            weights = (jnp.exp2(block - row) + jnp.exp2(block - col)).astype(jnp.bfloat16)
            acc += jnp.dot(zr[t], weights, preferred_element_type=jnp.float32)
            radial += jnp.sum(
                (weights.astype(jnp.float32) * block).reshape(2 * TB // 8, 8, IB), axis=0
            )
            return acc, radial

        acc, radial = lax.fori_loop(
            0, n_t // 2, second_pass,
            (jnp.zeros((64, IB), jnp.float32), jnp.zeros((8, IB), jnp.float32)),
        )
        for q in range(4):
            k, cols = ic * 4 + q, slice(q * LANES, (q + 1) * LANES)
            msg[k, 0:64, :] = acc[:, cols]
            msg[k, 64:72, :] = radial[:, cols]
            if k > 0:
                send(f"P{k}", msg.at[k], precv.at[k - 1], dev(*PLANE[k]))

    total = msg[0]
    for k in range(len(PLANE) - 1, 0, -1):
        recv(f"P{k}", precv.at[k - 1])
        total += precv[k - 1]
    pulled = 50.0 * total[0:64] - 100.0 * own_zr
    radial = (0.5 / LOG2E) * jnp.sum(total[64:72], axis=0, keepdims=True) - own_logit
    gall[feat] = (pulled - radial * izr) / norm

    for dx, dy in mates:
        send(f"g{dx}{dy}", gall.at[feat], gall.at[feat], dev(dx, dy))

    def mate(dx, dy):
        return x_part[-dx % X] + y_feat[-dy % Y]

    for dx, dy in mates:
        came = mate(dx, dy)
        recv(f"m{dx}{dy}", maskall.at[:, pl.ds(pl.multiple_of(came * pairs, pairs), pairs)])
        recv(f"r{dx}{dy}", frecv.at[came])
    for dx, dy in mates:
        recv(f"g{dx}{dy}", gall.at[mate(dx, dy)])

    shrink = 1.0 / math.sqrt(cfg["vw"])
    for f in range(2 * X):
        g = gall[f]
        for a in range(8):
            phi[a * 64 : (a + 1) * 64, f * pairs : (f + 1) * pairs] = (
                frecv[f, a : a + 1, :] * g * shrink
            ).astype(jnp.bfloat16)
    summed = dot_nt(maskall[...], phi[...])
    high = summed.astype(jnp.bfloat16)
    rest = summed - high.astype(jnp.float32)
    mid = rest.astype(jnp.bfloat16)
    low = (rest - mid.astype(jnp.float32)).astype(jnp.bfloat16)
    tests = tg[...]
    scores = dot_nt(high, tests) + (dot_nt(mid, tests) + dot_nt(low, tests))
    tot[...] = scores.reshape(tot.shape)

    send("core", tot.at[:, :, 1 - c], crecv, dev(0, 0, 0, 1))
    recv("core", crecv)
    both = tot[:, :, c] + crecv[...]
    lane = lax.broadcasted_iota(jnp.int32, (HZ * 8, LANES), 1)
    for ylow in range(2):
        low_z = both[ylow, :HZ].reshape(HZ * 8, -1)
        high_z = both[ylow, HZ:].reshape(HZ * 8, -1)
        for xx in range(X):
            cols = slice(xx * LANES, (xx + 1) * LANES)
            a, b = low_z[:, cols], high_z[:, cols]
            first = jnp.where(lane < 64, a, pltpu.roll(b, 64, 1))
            second = jnp.where(lane < 64, pltpu.roll(a, 64, 1), b)
            pk[xx * Y + ylow] = first.reshape(HZ, 8, LANES)
            pk[xx * Y + 2 + ylow] = second.reshape(HZ, 8, LANES)
    for k, (dx, dy) in enumerate(plane):
        send(f"Q{k}", pk.at[image_slot(dx, dy)], prs.at[k], dev(dx, dy))
    total = pk[image_slot(0, 0)]
    for k in range(len(plane)):
        recv(f"Q{k}", prs.at[k])
        total += prs[k]
    acc2[...] = total
    for dz in range(1, Z):
        send(f"Z{dz}", acc2.at[zs[dz] & (HZ - 1)], zrs.at[dz - 1], dev(0, 0, dz, 0))
    total = acc2[z & (HZ - 1)]
    for dz in range(1, Z):
        recv(f"Z{dz}", zrs.at[dz - 1])
        total += zrs[dz - 1]
    total = jnp.where(z >= HZ, pltpu.roll(total, 64, 1), total)
    out_ref[...] = total[:, :64] * (1.0 / cfg["divide"])
    drain()


def on_device(*args):
    image_feats, text_feats, image_head, text_head, sign_image, sign_embed, tests, masks = args
    pairs, vw = image_feats.shape
    width = image_head.shape[1]
    Z = lax.axis_size("dp") // 4
    n_devices = lax.axis_size("dp") * lax.axis_size("feat")
    cfg = {"pairs": pairs, "Z": Z, "vw": vw, "divide": math.sqrt(pairs * n_devices * 4096)}
    n_image, n_text = X * Y * pairs, 2 * Z * pairs
    subsets, n_tests = masks.shape[0], tests.shape[0]
    f32, bf16 = jnp.float32, jnp.bfloat16
    vmem = pltpu.VMEM
    operands = (
        image_feats, text_feats, image_head, text_head, sign_image.T, sign_embed.T, masks, tests,
    )
    n_copies = 40 + 4 * Z - 2 + Z + 15 + 2 * Z - 1 + 15 + 21 + 1 + 15 + Z - 1
    scratch = [vmem(value.shape, value.dtype) for value in operands] + [
        vmem((64, width), bf16),
        vmem((n_image, width), bf16),
        vmem((n_text, width), bf16),
        vmem((X * Y // 4, n_text, 4 * pairs), f32),
        vmem((n_text // (4 * pairs), 64, 4 * pairs), bf16),
        vmem((n_text, LANES), f32),
        vmem((n_text, LANES), f32),
        vmem((X * Y // 4, 8, 4 * pairs), f32),
        vmem((X * Y // 4, 8, 4 * pairs), f32),
        vmem((X * Y, X * Y, pairs), f32),
        vmem((2 * Z, 2 * Z, pairs), f32),
        vmem((X * Y // 4, 1, 4 * pairs), f32),
        vmem((X * Y, 72, pairs), f32),
        vmem((X * Y - 1, 72, pairs), f32),
        vmem((64, pairs), f32),
        vmem((2 * X, 64, pairs), f32),
        vmem((2 * X, 8, pairs), f32),
        vmem((subsets, 2 * X * pairs), bf16),
        vmem((512, 2 * X * pairs), bf16),
        vmem((2, Z, 2, 8, n_tests), f32),
        vmem((2, Z, 8, n_tests), f32),
        vmem((X * Y, Z // 2, 8, LANES), f32),
        vmem((X * Y - 1, Z // 2, 8, LANES), f32),
        vmem((Z // 2, 8, LANES), f32),
        vmem((Z - 1, 8, LANES), f32),
        pltpu.SemaphoreType.DMA((n_copies,)),
        pltpu.SemaphoreType.DMA((n_copies,)),
        pltpu.SemaphoreType.DMA((len(operands),)),
    ]
    return pl.pallas_call(
        functools.partial(kernel, cfg),
        out_shape=jax.ShapeDtypeStruct((8, 64), f32),
        in_specs=[pl.BlockSpec(memory_space=pl.ANY)] * len(operands),
        out_specs=pl.BlockSpec(memory_space=pltpu.VMEM),
        scratch_shapes=scratch,
        compiler_params=pltpu.CompilerParams(
            collective_id=0, has_side_effects=True, vmem_limit_bytes=60 * 1024 * 1024
        ),
    )(*operands)


def solution(mesh):
    placed = (
        P(("dp", "feat"), None),
        P(("dp", "feat"), None),
        P(),
        P(),
        P(),
        P(),
        P(None, "feat"),
        P(None, ("dp", "feat")),
    )
    return jax.shard_map(
        on_device, mesh=mesh, in_specs=placed, out_specs=P("dp", "feat"), check_vma=False
    )
```

profile of v0, /device:TPU:1, one launch (start us, length us, event | category | flops | bytes accessed | tf_op | source)
XLA Modules:
  0.0 104.3 jit_solution(13298475240751120864)
XLA Ops:
  0.0 103.0 %shard_map.82 = f32[8,64]{1,0:T(8,128)} custom-call(bf16[128,1664]{1,0:T(8,128)(2,1)} %feats_hbm.1, bf16[128,1280]{1,0:T(8,128)(2,1)} %tfeats_hbm.1, bf16[1664,1280]{1,0:T(8,128)(2,1)} %ihead_hbm.1, bf16[1280,1280]{1,0:T(8,128)(2,1)} %thead_hbm.1, s32[64,1664]{1,0:T(8,128)} %bitcast.2, s32[64,1280]{1,0:T(8,128)} %bitcast.3, s32[256,128]{1,0:T(8,128)} %mask_hbm.1, ...), custom_call_target="tpu_custom_call" | custom-call | tf_op jit(solution)/shard_map/pallas_call | solution.py:521
  103.0 1.3 %copy.10 = f32[8,64]{1,0:T(8,128)} copy(f32[8,64]{1,0:T(8,128)} %shard_map.82) | data formatting | bytes 4096
where the time goes:
time: 104 us
  Pallas kernels  103 us (99%)
  local copies, waits for them, and re-layouts  1.28 us (1%)
    pallas_call x1, Pallas kernels, on_device(): pl.pallas_call(functools.partial(kernel, cfg), out_shape=jax.ShapeDtypeSt...  103 us

commit v1 on v0

--- a/solution.py
+++ b/solution.py
@@ -83,16 +83,22 @@
     def text_slot(dz, dc):
         return cs[dc % 2] * Z + zs[dz % Z]
 
-    plane = PLANE[1:]
-    line = [(dz, dc) for dc in range(2) for dz in range(Z) if (dz, dc) != (0, 0)]
-    mates = [(dx, 2 * h) for dx in range(X) for h in range(2) if (dx, h) != (0, 0)]
+    plane = PLANE[:0:-1]
+    line = order[:0:-1]
+    mates = [(2, 1), (1, 1), (-1, 1), (2, 0), (0, 1), (1, 0), (-1, 0)]
+
+    def mate(dx, h):
+        return {
+            "dp": ((yl ^ h) << Z.bit_length()) + z_part[0] + c,
+            "feat": x_part[dx % X] + (y_feat[0] ^ h),
+        }
 
     loads = [
         pltpu.make_async_copy(src, dst, load_sem.at[i])
         for i, (src, dst) in enumerate(
             (
-                (tfeats_hbm, tfeats), (thead_hbm, thead), (feats_hbm, feats),
-                (ihead_hbm, ihead), (signe_hbm, signe), (signi_hbm, signi),
+                (feats_hbm, feats), (ihead_hbm, ihead), (tfeats_hbm, tfeats),
+                (thead_hbm, thead), (signe_hbm, signe), (signi_hbm, signi),
                 (mask_hbm, masks), (tg_hbm, tg),
             )
         )
@@ -101,10 +107,11 @@
         load.start()
 
     barrier = pltpu.get_barrier_semaphore()
-    for dx, dy in plane:
-        pl.semaphore_signal(barrier, inc=1, device_id=dev(dx, dy), device_id_type=MESH)
-    for dz, dc in line:
-        pl.semaphore_signal(barrier, inc=1, device_id=dev(0, 0, dz, dc), device_id_type=MESH)
+    near = [(0, 0, 0, 1)]
+    for d in (1, -1):
+        near += [(d, 0, 0, 0), (0, d, 0, 0), (0, 0, d, 0)]
+    for offsets in near:
+        pl.semaphore_signal(barrier, inc=1, device_id=dev(*offsets), device_id_type=MESH)
 
     names = Names()
     started = []
@@ -215,17 +222,20 @@
 
     scale = 100.0 * LOG2E
 
-    def tile(t, ic):
+    def tile(t, ic, h=None):
         rows = pl.ds(t * TB if isinstance(t, int) else pl.multiple_of(t * TB, TB), TB)
-        cols = pl.ds(ic * IB if isinstance(ic, int) else pl.multiple_of(ic * IB, IB), IB)
-        block = dot_nt(txt[rows, :], img[cols, :]) * scale
-        logit[ic, rows, :] = block
-        deep = block.reshape(TB // 8, 8, IB)
-        old = imax[ic]
+        width = IB if h is None else IB // 2
+        c0 = 0 if h is None else h * width
+        cols = slice(c0, c0 + width)
+        block = dot_nt(txt[rows, :], img[ic * IB + c0 : ic * IB + c0 + width, :]) * scale
+        logit[ic, rows, cols] = block
+        deep = block.reshape(TB // 8, 8, width)
+        old = imax[ic, :, cols]
         new = jnp.maximum(old, jnp.max(deep, axis=0))
-        isum[ic] = isum[ic] * jnp.exp2(old - new) + jnp.sum(jnp.exp2(deep - new[None]), axis=0)
-        imax[ic] = new
-        parts = [block[:, k : k + LANES] for k in range(0, IB, LANES)]
+        total = jnp.sum(jnp.exp2(deep - new[None]), axis=0)
+        isum[ic, :, cols] = isum[ic, :, cols] * jnp.exp2(old - new) + total
+        imax[ic, :, cols] = new
+        parts = [block[:, k : k + LANES] for k in range(0, width, LANES)]
         old = tmax[rows, :]
         new = functools.reduce(jnp.maximum, parts, old)
         tsum[rows, :] = functools.reduce(
@@ -237,8 +247,8 @@
 
     def tiles(n, at_step):
         def body(i, carry):
-            for t, ic in at_step(i):
-                tile(t, ic)
+            for args in at_step(i):
+                tile(*args)
             return carry
 
         lax.fori_loop(0, n, body, 0)
@@ -247,20 +257,20 @@
 
     loads[0].wait()
     loads[1].wait()
+    own_image, length = project(feats, ihead)
+    img[0:pairs, :] = own_image
+    pl.semaphore_wait(barrier, len(near))
+    for which in (0, 1):
+        first_send(which)
+    for which in (0, 1):
+        second_send(which, 0)
+    loads[2].wait()
+    loads[3].wait()
     own_text, _ = project(tfeats, thead)
     txt[0:pairs, :] = own_text
-    pl.semaphore_wait(barrier, len(plane) + len(line))
     text_send(0, 0)
     text_send(0, 1)
     text_share(0)
-    loads[2].wait()
-    loads[3].wait()
-    own_image, length = project(feats, ihead)
-    img[0:pairs, :] = own_image
-    for which in (0, 1):
-        first_send(which)
-    for which in (0, 1):
-        second_send(which, 0)
 
     for i in (4, 5, 6, 7):
         loads[i].wait()
@@ -299,20 +309,24 @@
     for dz in (0, 1, -1):
         text_shared(dz)
     tiles(3, lambda i: [(i, 0)])
-    for h in (0, 1):
-        text_recv(1, h)
-        text_send(2, h)
+    text_recv(1, 0)
+    text_send(2, 0)
+    text_recv(1, 1)
+    text_send(2, 1)
     text_share(2)
     text_share(-2)
     for which in (0, 1):
         for a in (-1, 1):
             second_forward(which, a)
+    tiles(3, lambda i: [(i, 1)])
+    text_recv(2, 0)
+    text_send(3, 0)
     text_shared(2)
     text_shared(-2)
     tiles(2, lambda i: [(i + 3, 0), (i + 3, 1)])
-    text_recv(2, 0)
-    text_send(3, 0)
-    tiles(3, lambda i: [(i, 1)])
+    for which in (0, 1):
+        second_last(which, 0)
+    tiles(2, lambda i: [(2 * i, 2, 0), (2 * i + 1, 2, 0)])
     text_recv(2, 1)
     text_send(3, 1)
     text_share(3)
@@ -322,24 +336,19 @@
     text_shared(3)
     text_shared(-3)
     tiles(2, lambda i: [(i + 5, 0), (i + 5, 1)])
-    for which in (0, 1):
-        for a in (0, 1):
-            second_last(which, a)
-    tiles(n_t - 1, lambda i: [(i, 2)])
+    tiles(1, lambda i: [(4, 2, 0), (5, 2, 0), (6, 2, 0)])
     text_recv(3, 0)
     text_recv(3, 1)
     text_share(HZ)
     for which in (0, 1):
-        for a in (-1, 2):
+        for a in (-1, 1):
             second_last(which, a)
-    tiles((n_t - 2) // 2, lambda i: [(2 * i, 3), (2 * i + 1, 3)])
+    tiles(n_t - 1, lambda i: [(i, 2, 1), (i, 3, 0)])
     text_shared(HZ)
-    tiles(1, lambda i: [(n_t - 2, 3), (n_t - 1, 0), (n_t - 1, 1), (n_t - 1, 2), (n_t - 1, 3)])
-
-    for dx, dy in mates:
-        to = dev(dx, dy)
-        send(f"m{dx}{dy}", maskall.at[:, mine], maskall.at[:, mine], to)
-        send(f"r{dx}{dy}", fbuf.at[pl.ds(to["feat"] * 8, 8), :], frecv.at[feat], to)
+    tiles(1, lambda i: [(7, 0), (7, 1), (7, 2), (7, 3, 0)])
+    for which in (0, 1):
+        second_last(which, 2)
+    tiles(n_t // 2, lambda i: [(2 * i, 3, 1), (2 * i + 1, 3, 1)])
 
     for k, (dx, dy) in enumerate(PLANE):
         ic, cols = k // 4, slice(k % 4 * LANES, (k % 4 + 1) * LANES)
@@ -356,8 +365,11 @@
         top = jnp.max(high, axis=0, keepdims=True)
         total = jnp.sum(tsum[rows, :].T * jnp.exp2(high - top), axis=0, keepdims=True)
         cbuf[0, pl.ds(text_slot(dz, dc), 1), :] = top + jnp.log2(total)
-    for k, (dz, dc) in enumerate(line):
-        send(f"C{k}", cbuf.at[0], cbuf.at[k + 1], dev(0, 0, dz, dc))
+    send("D", cbuf.at[0], cbuf.at[Z], dev(0, 0, 0, 1))
+    recv("D", cbuf.at[Z])
+    cbuf[Z + 1] = lse2([cbuf[0], cbuf[Z]])
+    for k, dz in enumerate(line):
+        send(f"C{k}", cbuf.at[Z + 1], cbuf.at[k + 1], dev(0, 0, dz, 0))
 
     for t in range(n_t // 2):
         rows = slice(t * 2 * TB, (t + 1) * 2 * TB)
@@ -372,10 +384,15 @@
         rows_lse[k // 4, :, cols] = rbuf[0, pl.ds(image_slot(dx, dy), 1), :]
     for k in range(len(line)):
         recv(f"C{k}", cbuf.at[k + 1])
-    cbuf[0] = lse2([cbuf[k] for k in range(len(line) + 1)])
+    cbuf[0] = lse2([cbuf[k] for k in (Z + 1, *range(1, Z))])
     for b, (dz, dc) in enumerate(texts):
         col = cbuf[0, pl.ds(text_slot(dz, dc), 1), :]
         tmax[b * LANES : (b + 1) * LANES, :] = jnp.broadcast_to(col, (LANES, LANES)).T
+
+    for dx, h in mates:
+        to = mate(dx, h)
+        send(f"m{dx}{h}", maskall.at[:, mine], maskall.at[:, mine], to)
+        send(f"r{dx}{h}", fbuf.at[pl.ds(to["feat"] * 8, 8), :], frecv.at[feat], to)
 
     for ic in (3, 2, 1, 0):
         row = rows_lse[ic]
@@ -412,18 +429,14 @@
     radial = (0.5 / LOG2E) * jnp.sum(total[64:72], axis=0, keepdims=True) - own_logit
     gall[feat] = (pulled - radial * izr) / norm
 
-    for dx, dy in mates:
-        send(f"g{dx}{dy}", gall.at[feat], gall.at[feat], dev(dx, dy))
-
-    def mate(dx, dy):
-        return x_part[-dx % X] + y_feat[-dy % Y]
-
-    for dx, dy in mates:
-        came = mate(dx, dy)
-        recv(f"m{dx}{dy}", maskall.at[:, pl.ds(pl.multiple_of(came * pairs, pairs), pairs)])
-        recv(f"r{dx}{dy}", frecv.at[came])
-    for dx, dy in mates:
-        recv(f"g{dx}{dy}", gall.at[mate(dx, dy)])
+    for dx, h in mates:
+        send(f"g{dx}{h}", gall.at[feat], gall.at[feat], mate(dx, h))
+    for dx, h in mates:
+        came = mate(-dx, h)["feat"]
+        recv(f"m{dx}{h}", maskall.at[:, pl.ds(pl.multiple_of(came * pairs, pairs), pairs)])
+        recv(f"r{dx}{h}", frecv.at[came])
+    for dx, h in mates:
+        recv(f"g{dx}{h}", gall.at[mate(-dx, h)["feat"]])
 
     shrink = 1.0 / math.sqrt(cfg["vw"])
     for f in range(2 * X):
@@ -455,14 +468,16 @@
             second = jnp.where(lane < 64, pltpu.roll(a, 64, 1), b)
             pk[xx * Y + ylow] = first.reshape(HZ, 8, LANES)
             pk[xx * Y + 2 + ylow] = second.reshape(HZ, 8, LANES)
+    own = image_slot(0, 0)
     for k, (dx, dy) in enumerate(plane):
         send(f"Q{k}", pk.at[image_slot(dx, dy)], prs.at[k], dev(dx, dy))
-    total = pk[image_slot(0, 0)]
+    total = pk[own]
     for k in range(len(plane)):
         recv(f"Q{k}", prs.at[k])
         total += prs[k]
     acc2[...] = total
-    for dz in range(1, Z):
+    for dz in line:
+        dz = dz % Z
         send(f"Z{dz}", acc2.at[zs[dz] & (HZ - 1)], zrs.at[dz - 1], dev(0, 0, dz, 0))
     total = acc2[z & (HZ - 1)]
     for dz in range(1, Z):
@@ -487,7 +502,7 @@
     operands = (
         image_feats, text_feats, image_head, text_head, sign_image.T, sign_embed.T, masks, tests,
     )
-    n_copies = 40 + 4 * Z - 2 + Z + 15 + 2 * Z - 1 + 15 + 21 + 1 + 15 + Z - 1
+    n_copies = 40 + 4 * Z - 2 + Z + 15 + Z + 15 + 21 + 1 + 15 + Z - 1
     scratch = [vmem(value.shape, value.dtype) for value in operands] + [
         vmem((64, width), bf16),
         vmem((n_image, width), bf16),
@@ -499,7 +514,7 @@
         vmem((X * Y // 4, 8, 4 * pairs), f32),
         vmem((X * Y // 4, 8, 4 * pairs), f32),
         vmem((X * Y, X * Y, pairs), f32),
-        vmem((2 * Z, 2 * Z, pairs), f32),
+        vmem((Z + 2, 2 * Z, pairs), f32),
         vmem((X * Y // 4, 1, 4 * pairs), f32),
         vmem((X * Y, 72, pairs), f32),
         vmem((X * Y - 1, 72, pairs), f32),

time: 104 us -> 99.2 us (0.954)
  Pallas kernels: 103 us -> 97.8 us
    pallas_call x1, Pallas kernels: 103 us -> 97.8 us  [on_device(): pl.pallas_call(functools.partial(kernel, cfg), out_shape=jax.ShapeDtypeSt...]
where the time goes in v1:
time: 99.2 us; the launch traced here: 99.1 us
  Pallas kernels  97.8 us (99%)
  local copies, waits for them, and re-layouts  1.28 us (1%)
    pallas_call x1, Pallas kernels, on_device(): pl.pallas_call(functools.partial(kernel, cfg), out_shape=jax.ShapeDtypeSt...  97.8 us

profile of v1, /device:TPU:1, one launch (start us, length us, event | category | flops | bytes accessed | tf_op | source)
XLA Modules:
  0.0 99.1 jit_solution(5373555462580730973)
XLA Ops:
  0.0 97.8 %shard_map.82 = f32[8,64]{1,0:T(8,128)} custom-call(bf16[128,1664]{1,0:T(8,128)(2,1)} %feats_hbm.1, bf16[128,1280]{1,0:T(8,128)(2,1)} %tfeats_hbm.1, bf16[1664,1280]{1,0:T(8,128)(2,1)} %ihead_hbm.1, bf16[1280,1280]{1,0:T(8,128)(2,1)} %thead_hbm.1, s32[64,1664]{1,0:T(8,128)} %bitcast.2, s32[64,1280]{1,0:T(8,128)} %bitcast.3, s32[256,128]{1,0:T(8,128)} %mask_hbm.1, ...), custom_call_target="tpu_custom_call" | custom-call | tf_op jit(solution)/shard_map/pallas_call | solution.py:536
  97.8 1.3 %copy.10 = f32[8,64]{1,0:T(8,128)} copy(f32[8,64]{1,0:T(8,128)} %shard_map.82) | data formatting | bytes 4096

commit v2 on v1

--- a/solution.py
+++ b/solution.py
@@ -47,7 +47,7 @@
     out_ref,
     feats, tfeats, ihead, thead, signi, signe, masks, tg,
     sgne, img, txt, logit, zr, tmax, tsum, imax, isum, rbuf, cbuf, rows_lse, msg, precv,
-    fbuf, gall, frecv, maskall, phi, tot, crecv, pk, prs, acc2, zrs,
+    fbuf, gmsg, gall, maskall, phi, tot, crecv, pk, prs, acc2, zrs,
     send_sem, recv_sem, load_sem,
 ):
     pairs, Z, TB = cfg["pairs"], cfg["Z"], 2 * cfg["pairs"]
@@ -155,20 +155,25 @@
 
     def text_pieces(s, up):
         if s < HZ - 1:
-            return (0, 1)
-        return (0,) if up else (1,)
-
-    def text_send(s, h):
+            return (0, 1, 2, 3)
+        return (0, 1) if up else (2, 3)
+
+    def text_send(s, q):
         for up, step in ((True, 1), (False, -1)):
-            if h in text_pieces(s, up):
-                src = text(-s * step, 0, h * half, half)
-                dst = text(-(s + 1) * step, 0, h * half, half)
-                send(f"z{step}{s}{h}", src, dst, dev(0, 0, step, 0))
-
-    def text_recv(s, h):
+            if q in text_pieces(s, up):
+                src = text(-s * step, 0, q * quarter, quarter)
+                dst = text(-(s + 1) * step, 0, q * quarter, quarter)
+                send(f"z{step}{s}{q}", src, dst, dev(0, 0, step, 0))
+
+    def text_recv(s, q):
         for up, step in ((True, 1), (False, -1)):
-            if h in text_pieces(s, up):
-                recv(f"z{step}{s}{h}", text(-(s + 1) * step, 0, h * half, half))
+            if q in text_pieces(s, up):
+                recv(f"z{step}{s}{q}", text(-(s + 1) * step, 0, q * quarter, quarter))
+
+    def text_next(s, *qs):
+        for q in qs:
+            text_recv(s, q)
+            text_send(s + 1, q)
 
     def text_share(dz):
         send(f"s{dz}", text(dz, 0, 0, pairs), text(dz, 1, 0, pairs), dev(0, 0, 0, 1))
@@ -268,8 +273,8 @@
     loads[3].wait()
     own_text, _ = project(tfeats, thead)
     txt[0:pairs, :] = own_text
-    text_send(0, 0)
-    text_send(0, 1)
+    for q in range(4):
+        text_send(0, q)
     text_share(0)
 
     for i in (4, 5, 6, 7):
@@ -286,7 +291,6 @@
     fbuf[...] = dot_nt((2 * signi[...] - 1).astype(jnp.bfloat16), feats[...])
     mine = pl.ds(pl.multiple_of(feat * pairs, pairs), pairs)
     maskall[:, mine] = masks[...].astype(jnp.bfloat16)
-    frecv[feat] = fbuf[pl.ds(pl.multiple_of(feat * 8, 8), 8), :]
     tmax[...] = jnp.full(tmax.shape, -1e30, jnp.float32)
     tsum[...] = jnp.zeros(tsum.shape, jnp.float32)
     imax[...] = jnp.full(imax.shape, -1e30, jnp.float32)
@@ -296,59 +300,61 @@
         first_forward(which)
         second_send(which, -1)
         second_send(which, 1)
-    for h in (0, 1):
-        text_recv(0, h)
-        text_send(1, h)
+    text_next(0, 0, 1)
+    for which in (0, 1):
+        second_forward(which, 0)
+    text_next(0, 2)
+    for which in (0, 1):
+        first_last(which)
+        second_send(which, 2)
+    text_next(0, 3)
     text_share(1)
     text_share(-1)
-    for which in (0, 1):
-        second_forward(which, 0)
-    for which in (0, 1):
-        first_last(which)
-        second_send(which, 2)
+    text_next(1, 0)
     for dz in (0, 1, -1):
         text_shared(dz)
-    tiles(3, lambda i: [(i, 0)])
-    text_recv(1, 0)
-    text_send(2, 0)
-    text_recv(1, 1)
-    text_send(2, 1)
+    tiles(1, lambda i: [(0, 0), (1, 0), (2, 0)])
+    text_next(1, 1)
+    for which in (0, 1):
+        second_forward(which, -1)
+    text_next(1, 2)
+    for which in (0, 1):
+        second_forward(which, 1)
+    text_next(1, 3)
     text_share(2)
     text_share(-2)
-    for which in (0, 1):
-        for a in (-1, 1):
-            second_forward(which, a)
-    tiles(3, lambda i: [(i, 1)])
-    text_recv(2, 0)
-    text_send(3, 0)
+    tiles(1, lambda i: [(0, 1), (1, 1), (2, 1)])
+    text_next(2, 0)
     text_shared(2)
     text_shared(-2)
-    tiles(2, lambda i: [(i + 3, 0), (i + 3, 1)])
+    tiles(1, lambda i: [(3, 0), (3, 1), (4, 0), (4, 1)])
+    text_next(2, 1)
+    for which in (0, 1):
+        second_forward(which, 2)
     for which in (0, 1):
         second_last(which, 0)
-    tiles(2, lambda i: [(2 * i, 2, 0), (2 * i + 1, 2, 0)])
-    text_recv(2, 1)
-    text_send(3, 1)
+    text_next(2, 2)
+    tiles(1, lambda i: [(t, 2, 0) for t in range(5)])
+    text_next(2, 3)
     text_share(3)
     text_share(-3)
-    for which in (0, 1):
-        second_forward(which, 2)
+    for dx, h in mates:
+        send(f"m{dx}{h}", maskall.at[:, mine], maskall.at[:, mine], mate(dx, h))
+    for which in (0, 1):
+        for a in (-1, 1):
+            second_last(which, a)
+    tiles(5, lambda i: [(i, 2, 1), (i, 3, 0)])
+    for q in range(4):
+        text_recv(HZ - 1, q)
+    text_share(HZ)
     text_shared(3)
     text_shared(-3)
-    tiles(2, lambda i: [(i + 5, 0), (i + 5, 1)])
-    tiles(1, lambda i: [(4, 2, 0), (5, 2, 0), (6, 2, 0)])
-    text_recv(3, 0)
-    text_recv(3, 1)
-    text_share(HZ)
-    for which in (0, 1):
-        for a in (-1, 1):
-            second_last(which, a)
-    tiles(n_t - 1, lambda i: [(i, 2, 1), (i, 3, 0)])
+    tiles(2, lambda i: [(i + 5, 0), (i + 5, 1), (i + 5, 2), (i + 5, 3, 0)])
+    for which in (0, 1):
+        second_last(which, 2)
+    tiles(1, lambda i: [(t, 3, 1) for t in range(7)])
     text_shared(HZ)
-    tiles(1, lambda i: [(7, 0), (7, 1), (7, 2), (7, 3, 0)])
-    for which in (0, 1):
-        second_last(which, 2)
-    tiles(n_t // 2, lambda i: [(2 * i, 3, 1), (2 * i + 1, 3, 1)])
+    tiles(1, lambda i: [(7, 0), (7, 1), (7, 2), (7, 3)])
 
     for k, (dx, dy) in enumerate(PLANE):
         ic, cols = k // 4, slice(k % 4 * LANES, (k % 4 + 1) * LANES)
@@ -389,11 +395,6 @@
         col = cbuf[0, pl.ds(text_slot(dz, dc), 1), :]
         tmax[b * LANES : (b + 1) * LANES, :] = jnp.broadcast_to(col, (LANES, LANES)).T
 
-    for dx, h in mates:
-        to = mate(dx, h)
-        send(f"m{dx}{h}", maskall.at[:, mine], maskall.at[:, mine], to)
-        send(f"r{dx}{h}", fbuf.at[pl.ds(to["feat"] * 8, 8), :], frecv.at[feat], to)
-
     for ic in (3, 2, 1, 0):
         row = rows_lse[ic]
 
@@ -427,23 +428,28 @@
         total += precv[k - 1]
     pulled = 50.0 * total[0:64] - 100.0 * own_zr
     radial = (0.5 / LOG2E) * jnp.sum(total[64:72], axis=0, keepdims=True) - own_logit
-    gall[feat] = (pulled - radial * izr) / norm
-
-    for dx, h in mates:
-        send(f"g{dx}{h}", gall.at[feat], gall.at[feat], mate(dx, h))
+    grad = (pulled - radial * izr) / norm
+
+    def with_features(to):
+        return jnp.concatenate([grad, fbuf[pl.ds(pl.multiple_of(to * 8, 8), 8), :]], axis=0)
+
+    for k, (dx, h) in enumerate(mates):
+        to = mate(dx, h)
+        gmsg[k] = with_features(to["feat"])
+        send(f"g{dx}{h}", gmsg.at[k], gall.at[feat], to)
+    gall[feat] = with_features(feat)
     for dx, h in mates:
         came = mate(-dx, h)["feat"]
         recv(f"m{dx}{h}", maskall.at[:, pl.ds(pl.multiple_of(came * pairs, pairs), pairs)])
-        recv(f"r{dx}{h}", frecv.at[came])
     for dx, h in mates:
         recv(f"g{dx}{h}", gall.at[mate(-dx, h)["feat"]])
 
     shrink = 1.0 / math.sqrt(cfg["vw"])
     for f in range(2 * X):
-        g = gall[f]
+        g = gall[f, 0:64]
         for a in range(8):
             phi[a * 64 : (a + 1) * 64, f * pairs : (f + 1) * pairs] = (
-                frecv[f, a : a + 1, :] * g * shrink
+                gall[f, 64 + a : 65 + a, :] * g * shrink
             ).astype(jnp.bfloat16)
     summed = dot_nt(maskall[...], phi[...])
     high = summed.astype(jnp.bfloat16)
@@ -502,7 +508,7 @@
     operands = (
         image_feats, text_feats, image_head, text_head, sign_image.T, sign_embed.T, masks, tests,
     )
-    n_copies = 40 + 4 * Z - 2 + Z + 15 + Z + 15 + 21 + 1 + 15 + Z - 1
+    n_copies = 40 + 4 * Z - 4 + Z + 15 + Z + 15 + 14 + 1 + 15 + Z - 1
     scratch = [vmem(value.shape, value.dtype) for value in operands] + [
         vmem((64, width), bf16),
         vmem((n_image, width), bf16),
@@ -519,8 +525,8 @@
         vmem((X * Y, 72, pairs), f32),
         vmem((X * Y - 1, 72, pairs), f32),
         vmem((64, pairs), f32),
-        vmem((2 * X, 64, pairs), f32),
-        vmem((2 * X, 8, pairs), f32),
+        vmem((2 * X - 1, 72, pairs), f32),
+        vmem((2 * X, 72, pairs), f32),
         vmem((subsets, 2 * X * pairs), bf16),
         vmem((512, 2 * X * pairs), bf16),
         vmem((2, Z, 2, 8, n_tests), f32),

time: 99.2 us -> 91.5 us (0.922)
  Pallas kernels: 97.8 us -> 90.1 us
    pallas_call x1, Pallas kernels: 97.8 us -> 90.1 us  [on_device(): pl.pallas_call(functools.partial(kernel, cfg), out_shape=jax.ShapeDtypeSt...]
where the time goes in v2:
time: 91.5 us; the launch traced here: 91.4 us
  Pallas kernels  90.1 us (98%)
  local copies, waits for them, and re-layouts  1.28 us (1%)
    pallas_call x1, Pallas kernels, on_device(): pl.pallas_call(functools.partial(kernel, cfg), out_shape=jax.ShapeDtypeSt...  90.1 us

profile of v2, /device:TPU:1, one launch (start us, length us, event | category | flops | bytes accessed | tf_op | source)
XLA Modules:
  0.0 91.4 jit_solution(13442608509043518243)
XLA Ops:
  0.0 90.1 %shard_map.82 = f32[8,64]{1,0:T(8,128)} custom-call(bf16[128,1664]{1,0:T(8,128)(2,1)} %feats_hbm.1, bf16[128,1280]{1,0:T(8,128)(2,1)} %tfeats_hbm.1, bf16[1664,1280]{1,0:T(8,128)(2,1)} %ihead_hbm.1, bf16[1280,1280]{1,0:T(8,128)(2,1)} %thead_hbm.1, s32[64,1664]{1,0:T(8,128)} %bitcast.2, s32[64,1280]{1,0:T(8,128)} %bitcast.3, s32[256,128]{1,0:T(8,128)} %mask_hbm.1, ...), custom_call_target="tpu_custom_call" | custom-call | tf_op jit(solution)/shard_map/pallas_call | solution.py:542
  90.1 1.3 %copy.10 = f32[8,64]{1,0:T(8,128)} copy(f32[8,64]{1,0:T(8,128)} %shard_map.82) | data formatting | bytes 4096

commit v3 on v2

--- a/solution.py
+++ b/solution.py
@@ -93,18 +93,25 @@
             "feat": x_part[dx % X] + (y_feat[0] ^ h),
         }
 
-    loads = [
-        pltpu.make_async_copy(src, dst, load_sem.at[i])
-        for i, (src, dst) in enumerate(
-            (
-                (feats_hbm, feats), (ihead_hbm, ihead), (tfeats_hbm, tfeats),
-                (thead_hbm, thead), (signe_hbm, signe), (signi_hbm, signi),
-                (mask_hbm, masks), (tg_hbm, tg),
-            )
-        )
-    ]
-    for load in loads:
-        load.start()
+    loads = []
+
+    def load(src, dst):
+        copy = pltpu.make_async_copy(src, dst, load_sem.at[len(loads)])
+        copy.start()
+        loads.append(copy)
+        return copy
+
+    def load_head(src, dst):
+        depth = src.shape[0]
+        cuts = [0, 3 * LANES, 6 * LANES, 9 * LANES, depth]
+        return [
+            (load(src.at[a:b, :], dst.at[a:b, :]), a, b)
+            for a, b in zip(cuts, cuts[1:])
+            if a < b
+        ]
+
+    feats_load = load(feats_hbm, feats)
+    ihead_loads = load_head(ihead_hbm, ihead)
 
     barrier = pltpu.get_barrier_semaphore()
     near = [(0, 0, 0, 1)]
@@ -112,6 +119,12 @@
         near += [(d, 0, 0, 0), (0, d, 0, 0), (0, 0, d, 0)]
     for offsets in near:
         pl.semaphore_signal(barrier, inc=1, device_id=dev(*offsets), device_id_type=MESH)
+
+    tfeats_load = load(tfeats_hbm, tfeats)
+    thead_loads = load_head(thead_hbm, thead)
+    other_loads = [
+        load(signe_hbm, signe), load(signi_hbm, signi), load(mask_hbm, masks), load(tg_hbm, tg)
+    ]
 
     names = Names()
     started = []
@@ -148,8 +161,15 @@
         k = order.index(wrap(dz, Z)) * 2 + dc % 2
         return txt.at[pl.ds(k * pairs + r0, n), :]
 
-    def project(feats_ref, head_ref):
-        proj = jnp.dot(feats_ref[...], head_ref[...], preferred_element_type=jnp.float32)
+    def project(feats_load, feats_ref, head_loads, head_ref):
+        feats_load.wait()
+        proj = None
+        for copy, a, b in head_loads:
+            copy.wait()
+            term = jnp.dot(
+                feats_ref[:, a:b], head_ref[a:b, :], preferred_element_type=jnp.float32
+            )
+            proj = term if proj is None else proj + term
         length = jnp.sqrt(jnp.sum(proj * proj, axis=1, keepdims=True) + 1e-06)
         return (proj / length).astype(jnp.bfloat16), length
 
@@ -227,14 +247,14 @@
 
     scale = 100.0 * LOG2E
 
-    def tile(t, ic, h=None):
-        rows = pl.ds(t * TB if isinstance(t, int) else pl.multiple_of(t * TB, TB), TB)
+    def tile(t, n, ic, h=None):
+        rows = slice(t * TB, (t + n) * TB)
         width = IB if h is None else IB // 2
         c0 = 0 if h is None else h * width
         cols = slice(c0, c0 + width)
         block = dot_nt(txt[rows, :], img[ic * IB + c0 : ic * IB + c0 + width, :]) * scale
         logit[ic, rows, cols] = block
-        deep = block.reshape(TB // 8, 8, width)
+        deep = block.reshape(n * TB // 8, 8, width)
         old = imax[ic, :, cols]
         new = jnp.maximum(old, jnp.max(deep, axis=0))
         total = jnp.sum(jnp.exp2(deep - new[None]), axis=0)
@@ -250,35 +270,27 @@
         )
         tmax[rows, :] = new
 
-    def tiles(n, at_step):
-        def body(i, carry):
-            for args in at_step(i):
-                tile(*args)
-            return carry
-
-        lax.fori_loop(0, n, body, 0)
+    def tiles(*steps):
+        for step in steps:
+            tile(*step)
 
     n_t = len(order)
 
-    loads[0].wait()
-    loads[1].wait()
-    own_image, length = project(feats, ihead)
+    own_image, length = project(feats_load, feats, ihead_loads, ihead)
     img[0:pairs, :] = own_image
     pl.semaphore_wait(barrier, len(near))
     for which in (0, 1):
         first_send(which)
     for which in (0, 1):
         second_send(which, 0)
-    loads[2].wait()
-    loads[3].wait()
-    own_text, _ = project(tfeats, thead)
+    own_text, _ = project(tfeats_load, tfeats, thead_loads, thead)
     txt[0:pairs, :] = own_text
     for q in range(4):
         text_send(0, q)
     text_share(0)
 
-    for i in (4, 5, 6, 7):
-        loads[i].wait()
+    for copy in other_loads:
+        copy.wait()
     sgne[...] = (2 * signe[...] - 1).astype(jnp.bfloat16)
     norm = jnp.broadcast_to(length, (pairs, LANES)).T[0:1, :]
     izr = dot_nt(sgne[...], own_image)
@@ -313,7 +325,7 @@
     text_next(1, 0)
     for dz in (0, 1, -1):
         text_shared(dz)
-    tiles(1, lambda i: [(0, 0), (1, 0), (2, 0)])
+    tiles((0, 1, 0), (1, 1, 0), (2, 1, 0))
     text_next(1, 1)
     for which in (0, 1):
         second_forward(which, -1)
@@ -323,18 +335,18 @@
     text_next(1, 3)
     text_share(2)
     text_share(-2)
-    tiles(1, lambda i: [(0, 1), (1, 1), (2, 1)])
+    tiles((0, 1, 1), (1, 1, 1), (2, 1, 1))
     text_next(2, 0)
     text_shared(2)
     text_shared(-2)
-    tiles(1, lambda i: [(3, 0), (3, 1), (4, 0), (4, 1)])
+    tiles((3, 1, 0), (3, 1, 1), (4, 1, 0), (4, 1, 1))
     text_next(2, 1)
     for which in (0, 1):
         second_forward(which, 2)
     for which in (0, 1):
         second_last(which, 0)
     text_next(2, 2)
-    tiles(1, lambda i: [(t, 2, 0) for t in range(5)])
+    tiles((0, 2, 2, 0), (2, 3, 2, 0))
     text_next(2, 3)
     text_share(3)
     text_share(-3)
@@ -343,18 +355,18 @@
     for which in (0, 1):
         for a in (-1, 1):
             second_last(which, a)
-    tiles(5, lambda i: [(i, 2, 1), (i, 3, 0)])
+    tiles((0, 2, 2, 1), (2, 3, 2, 1), (0, 2, 3, 0), (2, 3, 3, 0))
     for q in range(4):
         text_recv(HZ - 1, q)
     text_share(HZ)
     text_shared(3)
     text_shared(-3)
-    tiles(2, lambda i: [(i + 5, 0), (i + 5, 1), (i + 5, 2), (i + 5, 3, 0)])
+    tiles(*[(t, 1, ic) for t in (5, 6) for ic in range(3)], (5, 2, 3, 0))
     for which in (0, 1):
         second_last(which, 2)
-    tiles(1, lambda i: [(t, 3, 1) for t in range(7)])
     text_shared(HZ)
-    tiles(1, lambda i: [(7, 0), (7, 1), (7, 2), (7, 3)])
+    tiles((7, 1, 0), (7, 1, 1), (7, 1, 2), (7, 1, 3))
+    tiles((0, 2, 3, 1), (2, 2, 3, 1), (4, 3, 3, 1))
 
     for k, (dx, dy) in enumerate(PLANE):
         ic, cols = k // 4, slice(k % 4 * LANES, (k % 4 + 1) * LANES)
@@ -537,7 +549,7 @@
         vmem((Z - 1, 8, LANES), f32),
         pltpu.SemaphoreType.DMA((n_copies,)),
         pltpu.SemaphoreType.DMA((n_copies,)),
-        pltpu.SemaphoreType.DMA((len(operands),)),
+        pltpu.SemaphoreType.DMA((len(operands) + 6,)),
     ]
     return pl.pallas_call(
         functools.partial(kernel, cfg),

time: 91.5 us -> 90.4 us (0.988)
  Pallas kernels: 90.1 us -> 89 us
    pallas_call x1, Pallas kernels: 90.1 us -> 89 us  [on_device(): pl.pallas_call(functools.partial(kernel, cfg), out_shape=jax.ShapeDtypeSt...]
where the time goes in v3:
time: 90.4 us; the launch traced here: 90.2 us
  Pallas kernels  89 us (98%)
  local copies, waits for them, and re-layouts  1.28 us (1%)
    pallas_call x1, Pallas kernels, on_device(): pl.pallas_call(functools.partial(kernel, cfg), out_shape=jax.ShapeDtypeSt...  89 us

profile of v3, /device:TPU:1, one launch (start us, length us, event | category | flops | bytes accessed | tf_op | source)
XLA Modules:
  0.0 90.2 jit_solution(2182410494466726932)
XLA Ops:
  0.0 89.0 %shard_map.82 = f32[8,64]{1,0:T(8,128)} custom-call(bf16[128,1664]{1,0:T(8,128)(2,1)} %feats_hbm.1, bf16[128,1280]{1,0:T(8,128)(2,1)} %tfeats_hbm.1, bf16[1664,1280]{1,0:T(8,128)(2,1)} %ihead_hbm.1, bf16[1280,1280]{1,0:T(8,128)(2,1)} %thead_hbm.1, s32[64,1664]{1,0:T(8,128)} %bitcast.2, s32[64,1280]{1,0:T(8,128)} %bitcast.3, s32[256,128]{1,0:T(8,128)} %mask_hbm.1, ...), custom_call_target="tpu_custom_call" | custom-call | tf_op jit(solution)/shard_map/pallas_call | solution.py:554
  89.0 1.3 %copy.10 = f32[8,64]{1,0:T(8,128)} copy(f32[8,64]{1,0:T(8,128)} %shard_map.82) | data formatting | bytes 4096

commit v4 on v3

--- a/solution.py
+++ b/solution.py
@@ -47,7 +47,7 @@
     out_ref,
     feats, tfeats, ihead, thead, signi, signe, masks, tg,
     sgne, img, txt, logit, zr, tmax, tsum, imax, isum, rbuf, cbuf, rows_lse, msg, precv,
-    fbuf, gmsg, gall, maskall, phi, tot, crecv, pk, prs, acc2, zrs,
+    fbuf, gmsg, gall, maskall, phi, tot, csend, crecv, pk, prs, acc2, zrs,
     send_sem, recv_sem, load_sem,
 ):
     pairs, Z, TB = cfg["pairs"], cfg["Z"], 2 * cfg["pairs"]
@@ -368,6 +368,14 @@
     tiles((7, 1, 0), (7, 1, 1), (7, 1, 2), (7, 1, 3))
     tiles((0, 2, 3, 1), (2, 2, 3, 1), (4, 3, 3, 1))
 
+    texts = [(dz, dc) for dz in order for dc in range(2)]
+    for b, (dz, dc) in enumerate(texts):
+        rows = slice(b * LANES, (b + 1) * LANES)
+        high = tmax[rows, :].T
+        top = jnp.max(high, axis=0, keepdims=True)
+        total = jnp.sum(tsum[rows, :].T * jnp.exp2(high - top), axis=0, keepdims=True)
+        cbuf[0, pl.ds(text_slot(dz, dc), 1), :] = top + jnp.log2(total)
+    send("D", cbuf.at[0], cbuf.at[Z], dev(0, 0, 0, 1))
     for k, (dx, dy) in enumerate(PLANE):
         ic, cols = k // 4, slice(k % 4 * LANES, (k % 4 + 1) * LANES)
         high = imax[ic, :, cols]
@@ -376,14 +384,6 @@
         rbuf[0, pl.ds(image_slot(dx, dy), 1), :] = top + jnp.log2(total)
     for k, (dx, dy) in enumerate(plane):
         send(f"R{k}", rbuf.at[0], rbuf.at[k + 1], dev(dx, dy))
-    texts = [(dz, dc) for dz in order for dc in range(2)]
-    for b, (dz, dc) in enumerate(texts):
-        rows = slice(b * LANES, (b + 1) * LANES)
-        high = tmax[rows, :].T
-        top = jnp.max(high, axis=0, keepdims=True)
-        total = jnp.sum(tsum[rows, :].T * jnp.exp2(high - top), axis=0, keepdims=True)
-        cbuf[0, pl.ds(text_slot(dz, dc), 1), :] = top + jnp.log2(total)
-    send("D", cbuf.at[0], cbuf.at[Z], dev(0, 0, 0, 1))
     recv("D", cbuf.at[Z])
     cbuf[Z + 1] = lse2([cbuf[0], cbuf[Z]])
     for k, dz in enumerate(line):
@@ -464,17 +464,23 @@
                 gall[f, 64 + a : 65 + a, :] * g * shrink
             ).astype(jnp.bfloat16)
     summed = dot_nt(maskall[...], phi[...])
-    high = summed.astype(jnp.bfloat16)
-    rest = summed - high.astype(jnp.float32)
-    mid = rest.astype(jnp.bfloat16)
-    low = (rest - mid.astype(jnp.float32)).astype(jnp.bfloat16)
+    tot[...] = summed.reshape(tot.shape)
     tests = tg[...]
-    scores = dot_nt(high, tests) + (dot_nt(mid, tests) + dot_nt(low, tests))
-    tot[...] = scores.reshape(tot.shape)
-
-    send("core", tot.at[:, :, 1 - c], crecv, dev(0, 0, 0, 1))
+
+    def score(part):
+        high = part.astype(jnp.bfloat16)
+        rest = part - high.astype(jnp.float32)
+        mid = rest.astype(jnp.bfloat16)
+        low = (rest - mid.astype(jnp.float32)).astype(jnp.bfloat16)
+        return dot_nt(high, tests) + (dot_nt(mid, tests) + dot_nt(low, tests))
+
+    n_rows = 2 * Z * 8
+    theirs = score(tot[:, :, 1 - c].reshape(n_rows, -1))
+    csend[...] = theirs.reshape(csend.shape)
+    send("core", csend, crecv, dev(0, 0, 0, 1))
+    both = score(tot[:, :, c].reshape(n_rows, -1)).reshape(csend.shape)
     recv("core", crecv)
-    both = tot[:, :, c] + crecv[...]
+    both = both + crecv[...]
     lane = lax.broadcasted_iota(jnp.int32, (HZ * 8, LANES), 1)
     for ylow in range(2):
         low_z = both[ylow, :HZ].reshape(HZ * 8, -1)
@@ -541,7 +547,8 @@
         vmem((2 * X, 72, pairs), f32),
         vmem((subsets, 2 * X * pairs), bf16),
         vmem((512, 2 * X * pairs), bf16),
-        vmem((2, Z, 2, 8, n_tests), f32),
+        vmem((2, Z, 2, 8, 512), f32),
+        vmem((2, Z, 8, n_tests), f32),
         vmem((2, Z, 8, n_tests), f32),
         vmem((X * Y, Z // 2, 8, LANES), f32),
         vmem((X * Y - 1, Z // 2, 8, LANES), f32),

time: 90.4 us -> 91 us (level)
  no operation moved by 1% of the time
where the time goes in v4:
time: 91 us; the launch traced here: 90.8 us
  Pallas kernels  89.6 us (98%)
  local copies, waits for them, and re-layouts  1.28 us (1%)
    pallas_call x1, Pallas kernels, on_device(): pl.pallas_call(functools.partial(kernel, cfg), out_shape=jax.ShapeDtypeSt...  89.6 us

profile of v4, /device:TPU:1, one launch (start us, length us, event | category | flops | bytes accessed | tf_op | source)
XLA Modules:
  0.0 90.8 jit_solution(11694388106159193500)
XLA Ops:
  0.0 89.6 %shard_map.82 = f32[8,64]{1,0:T(8,128)} custom-call(bf16[128,1664]{1,0:T(8,128)(2,1)} %feats_hbm.1, bf16[128,1280]{1,0:T(8,128)(2,1)} %tfeats_hbm.1, bf16[1664,1280]{1,0:T(8,128)(2,1)} %ihead_hbm.1, bf16[1280,1280]{1,0:T(8,128)(2,1)} %thead_hbm.1, s32[64,1664]{1,0:T(8,128)} %bitcast.2, s32[64,1280]{1,0:T(8,128)} %bitcast.3, s32[256,128]{1,0:T(8,128)} %mask_hbm.1, ...), custom_call_target="tpu_custom_call" | custom-call | tf_op jit(solution)/shard_map/pallas_call | solution.py:561
  89.6 1.3 %copy.10 = f32[8,64]{1,0:T(8,128)} copy(f32[8,64]{1,0:T(8,128)} %shard_map.82) | data formatting | bytes 4096

commit v5 on v3

--- a/solution.py
+++ b/solution.py
@@ -426,6 +426,7 @@
         acc, radial = lax.fori_loop(
             0, n_t // 2, second_pass,
             (jnp.zeros((64, IB), jnp.float32), jnp.zeros((8, IB), jnp.float32)),
+            unroll=True,
         )
         for q in range(4):
             k, cols = ic * 4 + q, slice(q * LANES, (q + 1) * LANES)

time: 90.4 us -> 90 us (level)
  no operation moved by 1% of the time
where the time goes in v5:
time: 90 us; the launch traced here: 89.8 us
  Pallas kernels  88.6 us (98%)
  local copies, waits for them, and re-layouts  1.28 us (1%)
    pallas_call x1, Pallas kernels, on_device(): pl.pallas_call(functools.partial(kernel, cfg), out_shape=jax.ShapeDtypeSt...  88.6 us

profile of v5, /device:TPU:1, one launch (start us, length us, event | category | flops | bytes accessed | tf_op | source)
XLA Modules:
  0.0 89.8 jit_solution(17100485409094875408)
XLA Ops:
  0.0 88.6 %shard_map.82 = f32[8,64]{1,0:T(8,128)} custom-call(bf16[128,1664]{1,0:T(8,128)(2,1)} %feats_hbm.1, bf16[128,1280]{1,0:T(8,128)(2,1)} %tfeats_hbm.1, bf16[1664,1280]{1,0:T(8,128)(2,1)} %ihead_hbm.1, bf16[1280,1280]{1,0:T(8,128)(2,1)} %thead_hbm.1, s32[64,1664]{1,0:T(8,128)} %bitcast.2, s32[64,1280]{1,0:T(8,128)} %bitcast.3, s32[256,128]{1,0:T(8,128)} %mask_hbm.1, ...), custom_call_target="tpu_custom_call" | custom-call | tf_op jit(solution)/shard_map/pallas_call | solution.py:555
  88.6 1.3 %copy.10 = f32[8,64]{1,0:T(8,128)} copy(f32[8,64]{1,0:T(8,128)} %shard_map.82) | data formatting | bytes 4096
